TPU v7x, 32 devices: a whole 2x2x4 slice. The times are simulated.
32 devices in a mesh: belt: 8 (over z, core), mer: 4 (over y, x).
Axes of the slice: x: 2, y: 2, z: 4, core: 2. Of those that a mesh axis runs over, the one named last changes fastest.
Arguments:
- right_side: float32 [120, 32, 6144], P(None, 'mer', 'belt')
- helm_diag: float32 [120, 32, 6144], P(None, 'mer', 'belt'), may hold values from 1 to 3
- east_coef: float32 [120, 32, 6144], P(None, 'mer', 'belt'), may hold values from 0.5 to 1.5
- north_coef: float32 [120, 32, 6144], P(None, 'mer', 'belt'), may hold values from 0.5 to 1.5
- vert_coef: float32 [119, 32, 6144], P(None, 'mer', 'belt'), may hold values from 100 to 1000
- mortar_weights: float32 [8, 2], replicated, may hold values from 0.25 to 2
- weight_index: int32 [4, 32], replicated, may hold values from 0 to 7
- edge_map: int32 [4, 32, 2], replicated, may hold values from 0 to 31, as said below
- refined: int32 [4, 32], replicated, may hold values 0 or 1
Outputs:
- solution: float32 [120, 32, 6144], P(None, 'mer', 'belt')
- residual: float32 [120, 32, 6144], P(None, 'mer', 'belt')
Inputs may be any that keep to these rules, and one draw needn't show every extreme that they name: `edge_map`: for each edge and each of the two entries of a row, the 32 rows' entries form a permutation of the rows.
All inputs are finite; a program needn't handle non-finite values.
Results may differ from a plain program's by a relative error of at most 0.0003.
Values sent between devices are 32-bit elements; how exact they have to be, the bound alone decides.
A program may use at most 128 MiB of HBM per device.

v0:
```python
import functools

import jax
import jax.numpy as jnp
from jax import lax
from jax.experimental import pallas as pl
from jax.experimental.pallas import tpu as pltpu
from jax.sharding import PartitionSpec as P

LANES = 128
F32 = jnp.float32
MESH = pl.DeviceIdType.MESH
UNROLL = 4


def kernel(
    B, M, NB,
    rs_h, he_h, ea_h, no_h, ve_h, mw, wi, em, rf,
    sol_h, res_h,
    rs, he, ea, no, ve, pf, wf, im, jm, uu, iv,
    crow_s, crow_r, row_s, row_r, ccol_s, ccol_r, colw_s, colw_r, cole_s, cole_r,
    red1, red2,
    loc_sem, out_sem, crow_ss, crow_rs, row_ss, row_rs, ccol_sem, colw_sem, cole_ss, cole_rs,
    red1_ss, red1_rs, red2_ss, red2_rs,
):
    lev, rows, cols = rs.shape
    width = cols // NB
    per = width // LANES
    total_rows = wi.shape[1]
    nblk = cols // LANES
    b = lax.axis_index("belt")
    m = lax.axis_index("mer")
    per_panel = B // 4
    east_b = lax.rem(b + 1, B)
    west_b = lax.rem(b + B - 1, B)
    lane = lax.broadcasted_iota(jnp.int32, (rows, LANES), 1)
    sub = lax.broadcasted_iota(jnp.int32, (rows, LANES), 0)
    first_lane, last_lane = lane == 0, lane == LANES - 1
    first_row, last_row = sub == 0, sub == rows - 1
    zero = jnp.zeros((rows, LANES), F32)

    def at(j):
        return pl.ds(j * LANES, LANES)

    barrier = pltpu.get_barrier_semaphore()
    count = 0
    for d in range(1, B):
        pl.semaphore_signal(barrier, inc=1, device_id=(lax.rem(b + d, B), m), device_id_type=MESH)
        count += 1
    for d in range(1, M):
        other = lax.rem(m + d, M)
        for target in (b, east_b, west_b):
            pl.semaphore_signal(barrier, inc=1, device_id=(target, other), device_id_type=MESH)
            count += 1

    def load(which, src, dst, c):
        lanes = pl.ds(c * width, width)
        n = src.shape[0]
        return pltpu.make_async_copy(
            src.at[:, :, lanes], dst.at[pl.ds(0, n), :, lanes], loc_sem.at[which, c]
        )

    def loads(c):
        return [load(2, he_h, he, c), load(3, ve_h, ve, c), load(4, rs_h, rs, c)]

    for c in range(NB):
        load(0, no_h, no, c).start()
    for c in [NB - 1] + list(range(NB - 1)):
        load(1, ea_h, ea, c).start()
    for c in range(NB):
        for copy in loads(c):
            copy.start()
    ve[lev - 1] = jnp.zeros((rows, cols), F32)

    @pl.when(m == 0)
    def _():
        crow_r[...] = jnp.zeros(crow_r.shape, F32)
        row_r[:, 0] = jnp.zeros((2,) + row_r.shape[2:], F32)

    @pl.when(m == M - 1)
    def _():
        row_r[:, 1] = jnp.zeros((2,) + row_r.shape[2:], F32)

    def coef_row(c):
        return pltpu.make_async_remote_copy(
            src_ref=crow_s.at[c], dst_ref=crow_r.at[c], send_sem=crow_ss.at[c], recv_sem=crow_rs.at[c],
            device_id=(b, lax.rem(m + 1, M)), device_id_type=MESH)

    def field_row(f, side, c):
        to = lax.rem(m + 1, M) if side == 0 else lax.rem(m + M - 1, M)
        return pltpu.make_async_remote_copy(
            src_ref=row_s.at[f, side, c], dst_ref=row_r.at[f, side, c],
            send_sem=row_ss.at[f, side, c], recv_sem=row_rs.at[f, side, c],
            device_id=(b, to), device_id_type=MESH)

    def sends(copies_up, copies_down, what):
        @pl.when(m < M - 1)
        def _():
            for copy in copies_up:
                getattr(copy, what)()

        @pl.when(m > 0)
        def _():
            for copy in copies_down:
                getattr(copy, what)()

    coef_col = pltpu.make_async_remote_copy(
        src_ref=ccol_s, dst_ref=ccol_r, send_sem=ccol_sem.at[0], recv_sem=ccol_sem.at[1],
        device_id=(east_b, m), device_id_type=MESH)

    def last_col(f):
        return pltpu.make_async_remote_copy(
            src_ref=colw_s.at[f], dst_ref=colw_r.at[f], send_sem=colw_sem.at[f, 0], recv_sem=colw_sem.at[f, 1],
            device_id=(east_b, m), device_id_type=MESH)

    def first_cols(f):
        copies = []
        for d in range(M):
            copies.append(pltpu.make_async_remote_copy(
                src_ref=cole_s.at[f], dst_ref=cole_r.at[f, m], send_sem=cole_ss.at[f, d], recv_sem=cole_rs.at[f, m],
                device_id=(west_b, lax.rem(m + d, M)), device_id_type=MESH))
        return copies

    def first_col_wait(f, d):
        src = lax.rem(m + d, M)
        pltpu.make_async_remote_copy(
            src_ref=cole_s.at[f], dst_ref=cole_r.at[f, src], send_sem=cole_ss.at[f, d], recv_sem=cole_rs.at[f, src],
            device_id=(west_b, m), device_id_type=MESH).wait_recv()

    def level_loop(body, carry, reverse=False):
        def step(i, carry):
            for u in range(UNROLL):
                k = i * UNROLL + u
                if reverse:
                    k = lev - 1 - k
                carry = body(k, carry)
            return carry
        return lax.fori_loop(0, lev // UNROLL, step, carry)

    load(1, ea_h, ea, NB - 1).wait()

    def pack_coef(k, acc):
        return jnp.where(lane == k, pltpu.roll(ea[k, :, at(nblk - 1)], k + 1, 1), acc)

    ccol_s[...] = level_loop(pack_coef, zero)
    started = False
    for c in range(NB):
        load(0, no_h, no, c).wait()

        def pack_rows(k, _, c=c):
            for j in range(per):
                crow_s[c, j, pl.ds(k, 1), :] = no[k, pl.ds(rows - 1, 1), at(c * per + j)]
            return 0

        level_loop(pack_rows, 0)
        if not started:
            pl.semaphore_wait(barrier, count)
            coef_col.start()
            started = True
        sends([coef_row(c)], [], "start")

    e = b // per_panel
    lane_r = lax.broadcasted_iota(jnp.int32, (rows, total_rows), 1)
    sub_r = lax.broadcasted_iota(jnp.int32, (rows, total_rows), 0)
    own = lane_r == sub_r + m * rows
    maps = em[pl.ds(e, 1), pl.ds(pl.multiple_of(m * rows, rows), rows), :][0]
    pick_row = jnp.broadcast_to(wi[pl.ds(e, 1), :].astype(F32), (rows, total_rows))
    flag_row = jnp.broadcast_to(rf[pl.ds(e, 1), :].astype(F32), (rows, total_rows))
    pick = jnp.sum(jnp.where(own, pick_row, 0.0), axis=1, keepdims=True)
    flag = jnp.sum(jnp.where(own, flag_row, 0.0), axis=1, keepdims=True)
    at_edge = jnp.where(lax.rem(b + 1, per_panel) == 0, 1.0, 0.0)
    weights = jnp.zeros((rows, 2), F32)
    for j in range(mw.shape[0]):
        weights = jnp.where(pick == float(j), mw[j:j + 1, :], weights)
    mortar = jnp.where(lane_r == maps[:, 0:1], weights[:, 0:1], 0.0) + jnp.where(
        lane_r == maps[:, 1:2], weights[:, 1:2], 0.0)
    mortar = jnp.where(flag * at_edge > 0.5, mortar, jnp.where(own, 1.0, 0.0))

    def arrived_col(f):
        for d in range(M):
            first_col_wait(f, d)
        out = zero
        for s in range(total_rows):
            out = out + mortar[:, s:s + 1] * cole_r[f, s // rows, s % rows:s % rows + 1, :]
        return out

    def row_of(ref, k, j):
        return jnp.broadcast_to(ref[j, pl.ds(k, 1), :], (rows, LANES))

    def solve_back(c, f, field, get, put, extra, extra_body):
        c0 = c * per

        def body(k, carry):
            prev, packs, more = carry
            cur = []
            for j in range(per):
                z = iv[k, :, at(c0 + j)] * get[k, :, at(c0 + j)] + uu[k, :, at(c0 + j)] * prev[j]
                put[k, :, at(c0 + j)] = z
                row_s[f, 0, c, j, pl.ds(k, 1), :] = z[rows - 1:rows]
                row_s[f, 1, c, j, pl.ds(k, 1), :] = z[0:1]
                cur.append(z)
            lo, hi = packs
            if c == 0:
                lo = jnp.where(lane == k, pltpu.roll(cur[0], k, 1), lo)
            if c == NB - 1:
                hi = jnp.where(lane == k, pltpu.roll(cur[-1], k + 1, 1), hi)
            return tuple(cur), (lo, hi), extra_body(k, cur, more)

        _, (lo, hi), more = level_loop(body, ((zero,) * per, (zero, zero), extra), reverse=True)
        if c == 0:
            cole_s[f] = lo
            for copy in first_cols(f):
                copy.start()
        if c == NB - 1:
            colw_s[f] = hi
            last_col(f).start()
        sends([field_row(f, 0, c)], [field_row(f, 1, c)], "start")
        return more

    for c in [NB - 1] + list(range(NB - 1)):
        if c != NB - 1:
            load(1, ea_h, ea, c).wait()
    coef_col.wait_recv()
    for c in range(NB):
        for copy in loads(c):
            copy.wait()

        @pl.when(m > 0)
        def _():
            coef_row(c).wait_recv()

        c0 = c * per

        def factor(k, carry, c=c, c0=c0):
            v_prev, u_prev, g_prev = carry
            v_cur, u_cur, g_cur = [], [], []
            east = [ea[k, :, at(c0 + j)] for j in range(per)]
            turned = [pltpu.roll(x, 1, 1) for x in east]
            if c == 0:
                before = pltpu.roll(ccol_r[...], LANES - k, 1)
            else:
                before = pltpu.roll(ea[k, :, at(c0 - 1)], 1, 1)
            for j in range(per):
                north = no[k, :, at(c0 + j)]
                west = jnp.where(first_lane, before if j == 0 else turned[j - 1], turned[j])
                south = jnp.where(first_row, row_of(crow_r.at[c], k, j), pltpu.roll(north, 1, 0))
                up = ve[k, :, at(c0 + j)]
                diag = he[k, :, at(c0 + j)] + east[j] + west + north + south + up + v_prev[j]
                pivot = diag - v_prev[j] * u_prev[j]
                inverse = 1.0 / pivot
                u = up * inverse
                g = rs[k, :, at(c0 + j)] + u_prev[j] * g_prev[j]
                iv[k, :, at(c0 + j)] = inverse
                uu[k, :, at(c0 + j)] = u
                pf[k, :, at(c0 + j)] = g
                v_cur.append(up)
                u_cur.append(u)
                g_cur.append(g)
            return tuple(v_cur), tuple(u_cur), tuple(g_cur)

        level_loop(factor, ((zero,) * per,) * 3)
        solve_back(c, 0, None, pf, pf, 0, lambda k, cur, more: more)

    def horizontal(f, field, k, c, east_halo, west_halo):
        c0 = c * per
        v = [field[k, :, at(c0 + j)] for j in range(per)]
        east = [ea[k, :, at(c0 + j)] for j in range(per)]
        ahead = [pltpu.roll(x, LANES - 1, 1) for x in v]
        if c == NB - 1:
            ahead.append(pltpu.roll(east_halo, LANES - 1 - k, 1))
        else:
            ahead.append(pltpu.roll(field[k, :, at(c0 + per)], LANES - 1, 1))
        behind = [pltpu.roll(x * y, 1, 1) for x, y in zip(v, east)]
        if c == 0:
            behind.insert(0, pltpu.roll(west_halo, LANES - k, 1))
        else:
            behind.insert(0, pltpu.roll(field[k, :, at(c0 - 1)] * ea[k, :, at(c0 - 1)], 1, 1))
        out = []
        for j in range(per):
            north = no[k, :, at(c0 + j)]
            e_side = jnp.where(last_lane, ahead[j + 1], ahead[j])
            w_term = jnp.where(first_lane, behind[j], behind[j + 1])
            n_side = jnp.where(last_row, row_of(row_r.at[f, 1, c], k, j), pltpu.roll(v[j], rows - 1, 0))
            s_halo = row_of(row_r.at[f, 0, c], k, j) * row_of(crow_r.at[c], k, j)
            s_term = jnp.where(first_row, s_halo, pltpu.roll(north * v[j], 1, 0))
            out.append(east[j] * e_side + w_term + north * n_side + s_term)
        return v, out

    def wait_rows(f, c):
        @pl.when(m > 0)
        def _():
            field_row(f, 0, c).wait_recv()

        @pl.when(m < M - 1)
        def _():
            field_row(f, 1, c).wait_recv()

    last_col(0).wait_recv()
    east_halo = arrived_col(0)
    west_halo = colw_r[0] * ccol_r[...]
    rz, a00, a10, a01, a11 = zero, zero, zero, zero, zero
    for c in range(NB):
        wait_rows(0, c)
        c0 = c * per

        def image(k, carry, c=c, c0=c0):
            u_prev, g_prev, rz, a00 = carry
            u_cur, g_cur = [], []
            v, h = horizontal(0, pf, k, c, east_halo, west_halo)
            for j in range(per):
                r = rs[k, :, at(c0 + j)]
                x = r - h[j]
                g = x + u_prev[j] * g_prev[j]
                im[k, :, at(c0 + j)] = x
                wf[k, :, at(c0 + j)] = g
                rz = rz + r * v[j]
                a00 = a00 + x * v[j]
                u_cur.append(uu[k, :, at(c0 + j)])
                g_cur.append(g)
            return tuple(u_cur), tuple(g_cur), rz, a00

        _, _, rz, a00 = level_loop(image, ((zero,) * per, (zero,) * per, rz, a00))

        def dot(k, cur, more, c0=c0):
            for j in range(per):
                more = more + cur[j] * im[k, :, at(c0 + j)]
            return more

        a10 = solve_back(c, 1, None, wf, wf, a10, dot)

    last_col(1).wait_recv()
    east_halo = arrived_col(1)
    west_halo = colw_r[1] * ccol_r[...]
    for c in range(NB):
        wait_rows(1, c)
        c0 = c * per

        def second(k, carry, c=c, c0=c0):
            a01, a11 = carry
            v, h = horizontal(1, wf, k, c, east_halo, west_halo)
            for j in range(per):
                x = im[k, :, at(c0 + j)] - h[j]
                jm[k, :, at(c0 + j)] = x
                a01 = a01 + x * pf[k, :, at(c0 + j)]
                a11 = a11 + x * v[j]
            return a01, a11

        a01, a11 = level_loop(second, (a01, a11))

    tile = zero
    for i, acc in enumerate((rz, a00, a10, a01, a11)):
        tile = jnp.where(sub == i, jnp.sum(acc, axis=0, keepdims=True), tile)

    def exchange(buf, size, me, dev, ss, rs_, tile):
        buf[me] = tile
        copies = []
        for d in range(1, size):
            copies.append(pltpu.make_async_remote_copy(
                src_ref=buf.at[me], dst_ref=buf.at[me], send_sem=ss.at[d], recv_sem=rs_.at[me],
                device_id=dev(lax.rem(me + d, size)), device_id_type=MESH))
        for copy in copies:
            copy.start()
        for d in range(1, size):
            src = lax.rem(me + d, size)
            pltpu.make_async_remote_copy(
                src_ref=buf.at[me], dst_ref=buf.at[src], send_sem=ss.at[d], recv_sem=rs_.at[src],
                device_id=dev(src), device_id_type=MESH).wait_recv()
        out = buf[0]
        for i in range(1, size):
            out = out + buf[i]
        return out, copies

    tile, copies1 = exchange(red1, B, b, lambda i: (i, m), red1_ss, red1_rs, tile)
    tile, copies2 = exchange(red2, M, m, lambda i: (b, i), red2_ss, red2_rs, tile)
    sums = jnp.sum(tile, axis=1, keepdims=True)
    rz, a00, a10, a01, a11 = (sums[i:i + 1] for i in range(5))
    step0 = rz / a00
    rz1 = rz - 2.0 * step0 * a00 + step0 * step0 * a10
    grow = 1.0 + rz1 / rz
    curve = grow * grow * a00 - grow * step0 * (a01 + a10) + step0 * step0 * a11
    step1 = rz1 / curve
    along = jnp.broadcast_to(step0 + step1 * grow, (rows, LANES))
    back = jnp.broadcast_to(step1 * step0, (rows, LANES))

    outs = []
    for c in range(NB):
        c0 = c * per

        def finish(k, _, c0=c0):
            for j in range(per):
                s = at(c0 + j)
                iv[k, :, s] = along * pf[k, :, s] - back * wf[k, :, s]
                uu[k, :, s] = rs[k, :, s] - along * im[k, :, s] + back * jm[k, :, s]
            return 0

        level_loop(finish, 0)
        lanes = pl.ds(c * width, width)
        for i, (src, dst) in enumerate(((iv, sol_h), (uu, res_h))):
            copy = pltpu.make_async_copy(src.at[:, :, lanes], dst.at[:, :, lanes], out_sem.at[i, c])
            copy.start()
            outs.append(copy)

    coef_col.wait_send()
    for f in range(2):
        last_col(f).wait_send()
        for copy in first_cols(f):
            copy.wait_send()
    for c in range(NB):
        sends([coef_row(c), field_row(0, 0, c), field_row(1, 0, c)],
              [field_row(0, 1, c), field_row(1, 1, c)], "wait_send")
    for copy in copies1 + copies2:
        copy.wait_send()
    for copy in outs:
        copy.wait()


def on_device(B, M, right_side, helm_diag, east_coef, north_coef, vert_coef,
              mortar_weights, weight_index, edge_map, refined):
    lev, rows, cols = right_side.shape
    NB = 3
    width = cols // NB
    any_spec = pl.BlockSpec(memory_space=pl.ANY)
    vmem = pl.BlockSpec(memory_space=pltpu.VMEM)
    whole = pltpu.VMEM((lev, rows, cols), F32)
    tile = (rows, LANES)
    dma = pltpu.SemaphoreType.DMA
    return pl.pallas_call(
        functools.partial(kernel, B, M, NB),
        out_shape=(jax.ShapeDtypeStruct(right_side.shape, F32),) * 2,
        in_specs=[any_spec] * 5 + [vmem] * 4,
        out_specs=(any_spec, any_spec),
        scratch_shapes=[whole] * 11 + [
            pltpu.VMEM((NB, width // LANES, lev, LANES), F32),
            pltpu.VMEM((NB, width // LANES, lev, LANES), F32),
            pltpu.VMEM((2, 2, NB, width // LANES, lev, LANES), F32),
            pltpu.VMEM((2, 2, NB, width // LANES, lev, LANES), F32),
            pltpu.VMEM(tile, F32),
            pltpu.VMEM(tile, F32),
            pltpu.VMEM((2,) + tile, F32),
            pltpu.VMEM((2,) + tile, F32),
            pltpu.VMEM((2,) + tile, F32),
            pltpu.VMEM((2, M) + tile, F32),
            pltpu.VMEM((B,) + tile, F32),
            pltpu.VMEM((M,) + tile, F32),
            dma((5, NB)), dma((2, NB)), dma((NB,)), dma((NB,)), dma((2, 2, NB)), dma((2, 2, NB)),
            dma((2,)), dma((2, 2)), dma((2, M)), dma((2, M)),
            dma((B,)), dma((B,)), dma((M,)), dma((M,)),
        ],
        compiler_params=pltpu.CompilerParams(
            collective_id=0, has_side_effects=True, vmem_limit_bytes=56 * 1024 * 1024),
        cost_estimate=pl.CostEstimate(flops=60 * lev * rows * cols, bytes_accessed=28 * lev * rows * cols,
                                      transcendentals=0),
    )(right_side, helm_diag, east_coef, north_coef, vert_coef, mortar_weights, weight_index, edge_map, refined)


def solution(mesh):
    split = P(None, "mer", "belt")
    return jax.shard_map(
        functools.partial(on_device, mesh.shape["belt"], mesh.shape["mer"]),
        mesh=mesh,
        in_specs=(split,) * 5 + (P(),) * 4,
        out_specs=(split, split),
        check_vma=False,
    )
```

profile of v0, /device:TPU:0, one launch (start us, length us, event | category | flops | bytes accessed | tf_op | source)
XLA Modules:
  0.0 76.7 jit_solution(18241890556188164959)
XLA Ops:
  0.6 1.3 %copy.11.mw = f32[8,2]{1,0:T(8,128)} copy(f32[8,2]{0,1:T(2,128)} %param.14) | data formatting | bytes 128 | tf_op args[5]
  2.0 1.4 %copy.12.em = s32[4,32,2]{2,1,0:T(8,128)} copy(s32[4,32,2]{1,2,0:T(2,128)} %param.16) | data formatting | bytes 2048 | tf_op args[7]
  3.4 68.0 %shard_map.104 = (f32[120,8,768]{2,1,0:T(8,128)}, f32[120,8,768]{2,1,0:T(8,128)}) custom-call(f32[120,8,768]{2,1,0:T(8,128)} %rs_h.1, f32[120,8,768]{2,1,0:T(8,128)} %he_h.1, f32[120,8,768]{2,1,0:T(8,128)} %ea_h.1, f32[120,8,768]{2,1,0:T(8,128)} %no_h.1, f32[119,8,768]{2,1,0:T(8,128)} %ve_h.1, f32[8,2]{1,0:T(8,128)} %copy.11.mw, s32[4,32]{1,0:T(4,128)} %wi.1, ...), custom_call_target="tpu_custom_call" | custom-call | flops 44236800 | bytes 20643840 | tf_op jit(solution)/shard_map/pallas_call | solution.py:427
  71.3 0.0 copy-start
  71.4 3.8 %copy.15 = f32[120,8,768]{2,1,0:T(8,128)} copy(f32[120,8,768]{2,1,0:T(8,128)} %get-tuple-element.4) | data formatting | bytes 5898240
  75.1 0.0 copy-done
  75.1 1.6 %copy.16 = f32[120,8,768]{2,1,0:T(8,128)} copy(f32[120,8,768]{2,1,0:T(8,128)S(1)} %copy-done) | data formatting | bytes 5898240
Async XLA Ops:
  71.3 3.8 %copy-start = (f32[120,8,768]{2,1,0:T(8,128)S(1)}, f32[120,8,768]{2,1,0:T(8,128)}, u32[]{:S(2)}) copy-start(f32[120,8,768]{2,1,0:T(8,128)} %get-tuple-element.5) | copy-start | bytes 8847364
where the time goes:
time: 76.9 us; the launch traced here: 76.7 us
  Pallas kernels  68 us (88%)
  local copies, waits for them, and re-layouts  8.14 us (11%)
    pallas_call x1, Pallas kernels, on_device(): pl.pallas_call(functools.partial(kernel, B, M, NB), out_shape=(jax.ShapeD...  68 us
    unnamed x6, local copies, waits for them, and re-layouts  8.14 us

commit v1 on v0

--- a/solution.py
+++ b/solution.py
@@ -10,7 +10,7 @@
 LANES = 128
 F32 = jnp.float32
 MESH = pl.DeviceIdType.MESH
-UNROLL = 4
+UNROLL = 24
 
 
 def kernel(
@@ -163,17 +163,23 @@
     lane_r = lax.broadcasted_iota(jnp.int32, (rows, total_rows), 1)
     sub_r = lax.broadcasted_iota(jnp.int32, (rows, total_rows), 0)
     own = lane_r == sub_r + m * rows
-    maps = em[pl.ds(e, 1), pl.ds(pl.multiple_of(m * rows, rows), rows), :][0]
-    pick_row = jnp.broadcast_to(wi[pl.ds(e, 1), :].astype(F32), (rows, total_rows))
-    flag_row = jnp.broadcast_to(rf[pl.ds(e, 1), :].astype(F32), (rows, total_rows))
-    pick = jnp.sum(jnp.where(own, pick_row, 0.0), axis=1, keepdims=True)
-    flag = jnp.sum(jnp.where(own, flag_row, 0.0), axis=1, keepdims=True)
+    def own_entry(line):
+        line = jnp.broadcast_to(line.astype(F32), (rows, total_rows))
+        return jnp.sum(jnp.where(own, line, 0.0), axis=1, keepdims=True)
+
+    maps = em[pl.ds(e, 1), :, :][0]
+    first_map, second_map = own_entry(maps[0:1]), own_entry(maps[1:2])
+    pick = own_entry(wi[pl.ds(e, 1), :])
+    flag = own_entry(rf[pl.ds(e, 1), :])
     at_edge = jnp.where(lax.rem(b + 1, per_panel) == 0, 1.0, 0.0)
-    weights = jnp.zeros((rows, 2), F32)
-    for j in range(mw.shape[0]):
-        weights = jnp.where(pick == float(j), mw[j:j + 1, :], weights)
-    mortar = jnp.where(lane_r == maps[:, 0:1], weights[:, 0:1], 0.0) + jnp.where(
-        lane_r == maps[:, 1:2], weights[:, 1:2], 0.0)
+    entries = mw.shape[1]
+    picked = pick == lax.broadcasted_iota(jnp.int32, (rows, entries), 1).astype(F32)
+    weights = [
+        jnp.sum(jnp.where(picked, jnp.broadcast_to(mw[i:i + 1, :], (rows, entries)), 0.0), axis=1, keepdims=True)
+        for i in range(2)
+    ]
+    lane_f = lane_r.astype(F32)
+    mortar = jnp.where(lane_f == first_map, weights[0], 0.0) + jnp.where(lane_f == second_map, weights[1], 0.0)
     mortar = jnp.where(flag * at_edge > 0.5, mortar, jnp.where(own, 1.0, 0.0))
 
     def arrived_col(f):
@@ -417,7 +423,7 @@
 def on_device(B, M, right_side, helm_diag, east_coef, north_coef, vert_coef,
               mortar_weights, weight_index, edge_map, refined):
     lev, rows, cols = right_side.shape
-    NB = 3
+    NB = 2
     width = cols // NB
     any_spec = pl.BlockSpec(memory_space=pl.ANY)
     vmem = pl.BlockSpec(memory_space=pltpu.VMEM)
@@ -450,7 +456,8 @@
             collective_id=0, has_side_effects=True, vmem_limit_bytes=56 * 1024 * 1024),
         cost_estimate=pl.CostEstimate(flops=60 * lev * rows * cols, bytes_accessed=28 * lev * rows * cols,
                                       transcendentals=0),
-    )(right_side, helm_diag, east_coef, north_coef, vert_coef, mortar_weights, weight_index, edge_map, refined)
+    )(right_side, helm_diag, east_coef, north_coef, vert_coef,
+      mortar_weights.T, weight_index, edge_map.transpose(0, 2, 1), refined)
 
 
 def solution(mesh):

time: 76.9 us -> 67.1 us (0.87)
  Pallas kernels: 68 us -> 60.9 us
  local copies, waits for them, and re-layouts: 8.14 us -> 5.38 us
    pallas_call x1, Pallas kernels: 68 us -> 60.9 us  [on_device(): pl.pallas_call(functools.partial(kernel, B, M, NB), out_shape=(jax.ShapeD...]
    unnamed x6 -> x4, local copies, waits for them, and re-layouts: 8.14 us -> 5.38 us
where the time goes in v1:
time: 67.1 us; the launch traced here: 66.9 us
  Pallas kernels  60.9 us (91%)
  local copies, waits for them, and re-layouts  5.38 us (8%)
    pallas_call x1, Pallas kernels, on_device(): pl.pallas_call(functools.partial(kernel, B, M, NB), out_shape=(jax.ShapeD...  60.9 us
    unnamed x4, local copies, waits for them, and re-layouts  5.38 us

profile of v1, /device:TPU:0, one launch (start us, length us, event | category | flops | bytes accessed | tf_op | source)
XLA Modules:
  0.0 66.9 jit_solution(6791347106887889464)
XLA Ops:
  0.6 60.9 %shard_map.104 = (f32[120,8,768]{2,1,0:T(8,128)}, f32[120,8,768]{2,1,0:T(8,128)}) custom-call(f32[120,8,768]{2,1,0:T(8,128)} %rs_h.1, f32[120,8,768]{2,1,0:T(8,128)} %he_h.1, f32[120,8,768]{2,1,0:T(8,128)} %ea_h.1, f32[120,8,768]{2,1,0:T(8,128)} %no_h.1, f32[119,8,768]{2,1,0:T(8,128)} %ve_h.1, f32[2,8]{1,0:T(2,128)} %bitcast.3, s32[4,32]{1,0:T(4,128)} %wi.1, ...), custom_call_target="tpu_custom_call" | custom-call | flops 44236800 | bytes 20643840 | tf_op jit(solution)/shard_map/pallas_call | solution.py:433
  61.5 0.0 copy-start
  61.5 3.8 %copy.13 = f32[120,8,768]{2,1,0:T(8,128)} copy(f32[120,8,768]{2,1,0:T(8,128)} %get-tuple-element.4) | data formatting | bytes 5898240
  65.3 0.0 copy-done
  65.3 1.6 %copy.14 = f32[120,8,768]{2,1,0:T(8,128)} copy(f32[120,8,768]{2,1,0:T(8,128)S(1)} %copy-done) | data formatting | bytes 5898240
Async XLA Ops:
  61.5 3.8 %copy-start = (f32[120,8,768]{2,1,0:T(8,128)S(1)}, f32[120,8,768]{2,1,0:T(8,128)}, u32[]{:S(2)}) copy-start(f32[120,8,768]{2,1,0:T(8,128)} %get-tuple-element.5) | copy-start | bytes 8847364

commit v2 on v1

--- a/solution.py
+++ b/solution.py
@@ -19,9 +19,9 @@
     sol_h, res_h,
     rs, he, ea, no, ve, pf, wf, im, jm, uu, iv,
     crow_s, crow_r, row_s, row_r, ccol_s, ccol_r, colw_s, colw_r, cole_s, cole_r,
-    red1, red2,
+    red1, red2, rel,
     loc_sem, out_sem, crow_ss, crow_rs, row_ss, row_rs, ccol_sem, colw_sem, cole_ss, cole_rs,
-    red1_ss, red1_rs, red2_ss, red2_rs,
+    red1_ss, red1_rs, red2_ss, red2_rs, rel_ss, rel_rs,
 ):
     lev, rows, cols = rs.shape
     width = cols // NB
@@ -104,6 +104,62 @@
             for copy in copies_down:
                 getattr(copy, what)()
 
+    square = M == 4
+
+    def relayed(i, c):
+        return square and c == (NB - 1 if i == 0 else 0)
+
+    def to_corner(i, src, send_sem, corner):
+        return pltpu.make_async_remote_copy(
+            src_ref=src, dst_ref=rel.at[i], send_sem=send_sem, recv_sem=rel_rs.at[i],
+            device_id=(b, corner), device_id_type=MESH)
+
+    def from_corner(i, side):
+        c = NB - 1 if i == 0 else 0
+        dst = crow_r.at[c] if i == 0 else row_r.at[i - 1, side, c]
+        sem = crow_rs.at[c] if i == 0 else row_rs.at[i - 1, side, c]
+        return pltpu.make_async_remote_copy(
+            src_ref=rel.at[i], dst_ref=dst, send_sem=rel_ss.at[i], recv_sem=sem,
+            device_id=(b, 2 - side), device_id_type=MESH)
+
+    def forward(i, what):
+        if not square:
+            return
+        for side in range(1 if i == 0 else 2):
+            @pl.when(m == (3 if side == 0 else 0))
+            def _():
+                copy = from_corner(i, side)
+                if what == "start":
+                    to_corner(i, rel.at[i], rel_ss.at[i], 1).wait_recv()
+                getattr(copy, what)()
+
+    def start_coef(c):
+        if not relayed(0, c):
+            sends([coef_row(c)], [], "start")
+            return
+
+        @pl.when((m < M - 1) & (m != 1))
+        def _():
+            coef_row(c).start()
+
+        @pl.when(m == 1)
+        def _():
+            to_corner(0, crow_s.at[c], crow_ss.at[c], 3).start()
+
+    def start_rows(f, c):
+        if not relayed(f + 1, c):
+            sends([field_row(f, 0, c)], [field_row(f, 1, c)], "start")
+            return
+
+        for side, corner in ((0, 3), (1, 0)):
+            @pl.when((m != 1 + side) & (m != corner))
+            def _():
+                field_row(f, side, c).start()
+
+            @pl.when(m == 1 + side)
+            def _():
+                to_corner(f + 1, row_s.at[f, side, c], row_ss.at[f, side, c], corner).start()
+
     coef_col = pltpu.make_async_remote_copy(
         src_ref=ccol_s, dst_ref=ccol_r, send_sem=ccol_sem.at[0], recv_sem=ccol_sem.at[1],
         device_id=(east_b, m), device_id_type=MESH)
@@ -157,7 +213,7 @@
             pl.semaphore_wait(barrier, count)
             coef_col.start()
             started = True
-        sends([coef_row(c)], [], "start")
+        start_coef(c)
 
     e = b // per_panel
     lane_r = lax.broadcasted_iota(jnp.int32, (rows, total_rows), 1)
@@ -220,7 +276,7 @@
         if c == NB - 1:
             colw_s[f] = hi
             last_col(f).start()
-        sends([field_row(f, 0, c)], [field_row(f, 1, c)], "start")
+        start_rows(f, c)
         return more
 
     for c in [NB - 1] + list(range(NB - 1)):
@@ -230,6 +286,8 @@
     for c in range(NB):
         for copy in loads(c):
             copy.wait()
+        if c == NB - 1:
+            forward(0, "start")
 
         @pl.when(m > 0)
         def _():
@@ -301,6 +359,8 @@
         def _():
             field_row(f, 1, c).wait_recv()
 
+    forward(1, "start")
+
     last_col(0).wait_recv()
     east_halo = arrived_col(0)
     west_halo = colw_r[0] * ccol_r[...]
@@ -333,6 +393,8 @@
             return more
 
         a10 = solve_back(c, 1, None, wf, wf, a10, dot)
+
+    forward(2, "start")
 
     last_col(1).wait_recv()
     east_halo = arrived_col(1)
@@ -414,6 +476,8 @@
     for c in range(NB):
         sends([coef_row(c), field_row(0, 0, c), field_row(1, 0, c)],
               [field_row(0, 1, c), field_row(1, 1, c)], "wait_send")
+    for i in range(3):
+        forward(i, "wait_send")
     for copy in copies1 + copies2:
         copy.wait_send()
     for copy in outs:
@@ -448,9 +512,10 @@
             pltpu.VMEM((2, M) + tile, F32),
             pltpu.VMEM((B,) + tile, F32),
             pltpu.VMEM((M,) + tile, F32),
+            pltpu.VMEM((3, width // LANES, lev, LANES), F32),
             dma((5, NB)), dma((2, NB)), dma((NB,)), dma((NB,)), dma((2, 2, NB)), dma((2, 2, NB)),
             dma((2,)), dma((2, 2)), dma((2, M)), dma((2, M)),
-            dma((B,)), dma((B,)), dma((M,)), dma((M,)),
+            dma((B,)), dma((B,)), dma((M,)), dma((M,)), dma((3,)), dma((3,)),
         ],
         compiler_params=pltpu.CompilerParams(
             collective_id=0, has_side_effects=True, vmem_limit_bytes=56 * 1024 * 1024),

time: 67.1 us -> 66.1 us (0.985)
  Pallas kernels: 60.9 us -> 59.9 us
    pallas_call x1, Pallas kernels: 60.9 us -> 59.9 us  [on_device(): pl.pallas_call(functools.partial(kernel, B, M, NB), out_shape=(jax.ShapeD...]
where the time goes in v2:
time: 66.1 us; the launch traced here: 65.9 us
  Pallas kernels  59.9 us (91%)
  local copies, waits for them, and re-layouts  5.38 us (8%)
    pallas_call x1, Pallas kernels, on_device(): pl.pallas_call(functools.partial(kernel, B, M, NB), out_shape=(jax.ShapeD...  59.9 us
    unnamed x4, local copies, waits for them, and re-layouts  5.38 us

profile of v2, /device:TPU:0, one launch (start us, length us, event | category | flops | bytes accessed | tf_op | source)
XLA Modules:
  0.0 65.9 jit_solution(8846774605361472087)
XLA Ops:
  0.6 59.9 %shard_map.104 = (f32[120,8,768]{2,1,0:T(8,128)}, f32[120,8,768]{2,1,0:T(8,128)}) custom-call(f32[120,8,768]{2,1,0:T(8,128)} %rs_h.1, f32[120,8,768]{2,1,0:T(8,128)} %he_h.1, f32[120,8,768]{2,1,0:T(8,128)} %ea_h.1, f32[120,8,768]{2,1,0:T(8,128)} %no_h.1, f32[119,8,768]{2,1,0:T(8,128)} %ve_h.1, f32[2,8]{1,0:T(2,128)} %bitcast.3, s32[4,32]{1,0:T(4,128)} %wi.1, ...), custom_call_target="tpu_custom_call" | custom-call | flops 44236800 | bytes 20643840 | tf_op jit(solution)/shard_map/pallas_call | solution.py:497
  60.6 0.0 copy-start
  60.6 3.8 %copy.13 = f32[120,8,768]{2,1,0:T(8,128)} copy(f32[120,8,768]{2,1,0:T(8,128)} %get-tuple-element.4) | data formatting | bytes 5898240
  64.3 0.0 copy-done
  64.3 1.6 %copy.14 = f32[120,8,768]{2,1,0:T(8,128)} copy(f32[120,8,768]{2,1,0:T(8,128)S(1)} %copy-done) | data formatting | bytes 5898240
Async XLA Ops:
  60.6 3.8 %copy-start = (f32[120,8,768]{2,1,0:T(8,128)S(1)}, f32[120,8,768]{2,1,0:T(8,128)}, u32[]{:S(2)}) copy-start(f32[120,8,768]{2,1,0:T(8,128)} %get-tuple-element.5) | copy-start | bytes 8847364
